TPU v7x, 32 devices: a whole 2x2x4 slice. The times are simulated.
32 devices in a mesh: groups: 2 (over x), feat: 4 (over y, core), sub: 4 (over z).
Axes of the slice: x: 2, y: 2, z: 4, core: 2. Of those that a mesh axis runs over, the one named last changes fastest.
Arguments:
- hidden: bfloat16 [32, 8192], P('groups', 'feat'), parts along dimension 0, may hold values from -400 to 400
- input_norm_gain: bfloat16 [8192], P('feat'), may hold values from 0.25 to 1.75
- query_weight: bfloat16 [8192, 4096], P('feat', 'sub'), may hold values from -1 to 1
- key_weight: bfloat16 [8192, 512], P('feat', 'sub'), may hold values from -1 to 1
- value_weight: bfloat16 [8192, 512], P('feat', 'sub'), may hold values from -0.0625 to 0.0625
- adapter_down_weight: bfloat16 [8192, 512], P('feat'), may hold values from -0.0625 to 0.0625
- adapter_up_weight: bfloat16 [512, 4096], P(None, 'sub'), may hold values from -0.75 to 0.75
- output_weight: bfloat16 [4096, 8192], P('sub', 'feat'), may hold values from -0.09375 to 0.09375
- request_adapter: int32 [8], P('groups'), parts along dimension 0, may hold values from 0 to 7
- stored_owner: int32 [8, 4], P('groups'), parts along dimension 0, may hold values from 0 to 3, as said below
- stored_lengths: int32 [8], P('groups'), parts along dimension 0, may hold values from 2048 to 8192, as said below
- stored_keys: bfloat16 [16, 8192, 512], P(('groups', 'feat'), None, 'sub'), parts along dimension 0, may hold values from -400 to 400
- stored_values: bfloat16 [16, 8192, 512], P(('groups', 'feat'), None, 'sub'), parts along dimension 0, may hold values from -12 to 12
Outputs:
- attn_out: bfloat16 [32, 8192], P(('groups', 'sub'), 'feat'), parts along dimension 0
There are 2 independent parts, one for each index of `groups`. A program takes and returns all parts, laid end to end along the dimension named above; an argument that names none is the same for every part. Nothing has to cross between parts.
Inputs may be any that keep to these rules, and one draw needn't show every extreme that they name: `stored_owner`: for every key-value head no owner holds more than 2 requests, and some owner holds exactly 2. `stored_lengths`: some request has exactly 8192 cached tokens and some exactly 2048.
All inputs are finite; a program needn't handle non-finite values.
Results may differ from a plain program's by a relative error of at most 0.014.
Values may be sent and summed in bfloat16 or wider, within the bound.
A program may use at most 64 MiB of HBM per device.

v0:
```python
import jax
import jax.numpy as jnp
from jax import lax
from jax.sharding import PartitionSpec as P

MODEL_WIDTH = 8192
ADAPTER_RANK = 64
DRAFT = 4


norm_eps = 1e-05
rope_base = 500000.0


def rotate(values, positions):
    half_dim = values.shape[-1] // 2
    inv_freq = rope_base ** (-(jnp.arange(half_dim, dtype=jnp.float32) * 2.0) / values.shape[-1])
    angles = positions * inv_freq
    cosine = jnp.cos(angles)
    sine = jnp.sin(angles)
    first_half = values[..., :half_dim]
    second_half = values[..., half_dim:]
    return jnp.concatenate(
        [first_half * cosine - second_half * sine, second_half * cosine + first_half * sine],
        axis=-1,
    )


def body(
    hidden,
    input_norm_gain,
    query_weight,
    key_weight,
    value_weight,
    adapter_down_weight,
    adapter_up_weight,
    output_weight,
    request_adapter,
    stored_owner,
    stored_lengths,
    stored_keys,
    stored_values,
):
    feat_count = lax.axis_size("feat")
    my_feat = lax.axis_index("feat")
    my_head = lax.axis_index("sub")
    token_inputs = hidden.shape[0]
    query_cols = query_weight.shape[1]
    head_dim = key_weight.shape[1]
    group_size = query_cols // head_dim
    all_cols = query_cols + 2 * head_dim
    slot_count = stored_keys.shape[0]
    requests = request_adapter.shape[0]
    context = stored_keys.shape[1]
    hidden32 = hidden.astype(jnp.float32)
    squares = lax.psum(jnp.sum(hidden32 * hidden32, axis=1), "feat")
    normalized_hidden = (
        hidden32
        * lax.rsqrt(squares / MODEL_WIDTH + norm_eps)[:, None]
        * input_norm_gain.astype(jnp.float32)[None, :]
    ).astype(jnp.bfloat16)
    owner_col = lax.dynamic_slice_in_dim(stored_owner, my_head, 1, 1)[:, 0]
    req_iota = jnp.arange(requests)
    earlier = req_iota[None, :] < req_iota[:, None]
    same_owner = owner_col[None, :] == owner_col[:, None]
    slot_index = jnp.sum(jnp.logical_and(same_owner, earlier).astype(jnp.int32), axis=1)
    row_of = owner_col * slot_count + slot_index
    all_rows = jnp.arange(feat_count * slot_count)
    matches = row_of[None, :] == all_rows[:, None]
    slot_req = jnp.where(
        jnp.any(matches, axis=1), jnp.sum(jnp.where(matches, req_iota[None, :], 0), axis=1), -1
    )
    my_req = lax.dynamic_slice_in_dim(slot_req, my_feat * slot_count, slot_count, 0)
    draft_iota = jnp.arange(DRAFT)
    slot_tokens = jnp.where(
        slot_req[:, None] >= 0, slot_req[:, None] * DRAFT + draft_iota[None, :], -1
    ).reshape(-1)
    my_slot_tokens = lax.dynamic_slice_in_dim(
        slot_tokens, my_feat * slot_count * DRAFT, slot_count * DRAFT, 0
    )
    tok_iota = jnp.arange(token_inputs)
    tok_adapter = jnp.repeat(request_adapter, DRAFT)
    tok_position = jnp.repeat(stored_lengths, DRAFT) + jnp.tile(draft_iota, requests)
    column_adapter = jnp.arange(adapter_down_weight.shape[1]) // ADAPTER_RANK
    adapter_up_weight32 = adapter_up_weight.astype(jnp.float32)

    def adapter_match_mask(adapter_per_row):
        return column_adapter[None, :] == adapter_per_row[:, None]

    adapter_full = jnp.where(
        adapter_match_mask(tok_adapter),
        jnp.dot(normalized_hidden, adapter_down_weight, preferred_element_type=jnp.float32),
        0.0,
    )
    adapter_token = jnp.sum(adapter_full.reshape(token_inputs, -1, ADAPTER_RANK), axis=1)
    adapter_token = lax.psum(adapter_token, "feat")
    rows_dev = slot_count * DRAFT
    wanted = slot_tokens
    picks = wanted[:, None] == tok_iota[None, :]
    rows_x = jnp.dot(
        picks.astype(jnp.bfloat16), normalized_hidden, preferred_element_type=jnp.float32
    ).astype(jnp.bfloat16)
    adapter_per_row = jnp.where(
        wanted >= 0, jnp.sum(jnp.where(picks, tok_adapter[None, :], 0), axis=1), -1
    )
    query_part = jnp.dot(rows_x, query_weight, preferred_element_type=jnp.float32)
    key_part = jnp.dot(rows_x, key_weight, preferred_element_type=jnp.float32)
    value_part = jnp.dot(rows_x, value_weight, preferred_element_type=jnp.float32)
    sums = lax.psum_scatter(
        jnp.concatenate([query_part, key_part, value_part], axis=1),
        "feat",
        scatter_dimension=0,
        tiled=True,
    )
    selected_rows = my_slot_tokens[:, None] == tok_iota[None, :]
    query_total = sums[:, :query_cols]
    adapter_per_row = jnp.where(
        my_slot_tokens >= 0, jnp.sum(jnp.where(selected_rows, tok_adapter[None, :], 0), axis=1), -1
    )
    adapter_rows = jnp.dot(
        selected_rows.astype(jnp.float32), adapter_token, precision=lax.Precision.HIGHEST
    )
    widened_rows = jnp.where(
        adapter_match_mask(adapter_per_row),
        jnp.tile(adapter_rows, (1, column_adapter.shape[0] // ADAPTER_RANK)),
        0.0,
    )
    query_total = query_total + jnp.dot(
        widened_rows, adapter_up_weight32, precision=lax.Precision.HIGHEST
    )
    positions = jnp.sum(jnp.where(selected_rows, tok_position[None, :], 0), axis=1).astype(
        jnp.float32
    )
    query_rot = rotate(
        query_total.reshape(rows_dev, group_size, head_dim), positions[:, None, None]
    ).reshape(rows_dev, query_cols)
    key_rot = rotate(sums[:, query_cols : query_cols + head_dim], positions[:, None])
    packed = jnp.concatenate([query_rot, key_rot, sums[:, query_cols + head_dim :]], axis=1).astype(
        jnp.bfloat16
    )
    blocks = packed.reshape(slot_count, DRAFT, all_cols)
    query = blocks[:, :, :query_cols].reshape(slot_count, DRAFT, group_size, head_dim)
    key_new = blocks[:, :, query_cols : query_cols + head_dim]
    value_new = blocks[:, :, query_cols + head_dim :]
    slot_lengths = jnp.where(
        my_req >= 0,
        jnp.sum(
            jnp.where(my_req[:, None] == req_iota[None, :], stored_lengths[None, :], 0), axis=1
        ),
        0,
    )
    score_scale = head_dim ** (-0.5)
    cache_scores = (
        jnp.einsum("sdgx,scx->sdgc", query, stored_keys, preferred_element_type=jnp.float32)
        * score_scale
    )
    valid_cache = jnp.arange(context)[None, :] < slot_lengths[:, None]
    cache_scores = jnp.where(valid_cache[:, None, None, :], cache_scores, -1e30)
    new_scores = (
        jnp.einsum("sdgx,sex->sdge", query, key_new, preferred_element_type=jnp.float32)
        * score_scale
    )
    causal = draft_iota[None, :] <= draft_iota[:, None]
    new_scores = jnp.where(causal[None, :, None, :], new_scores, -1e30)
    row_max = jnp.maximum(jnp.max(cache_scores, axis=-1), jnp.max(new_scores, axis=-1))
    cache_exp = jnp.exp(cache_scores - row_max[..., None])
    new_exp = jnp.exp(new_scores - row_max[..., None])
    total = jnp.sum(cache_exp, axis=-1) + jnp.sum(new_exp, axis=-1)
    summed = jnp.einsum(
        "sdgc,scx->sdgx",
        cache_exp.astype(jnp.bfloat16),
        stored_values,
        preferred_element_type=jnp.float32,
    )
    summed = summed + jnp.einsum(
        "sdge,sex->sdgx",
        new_exp.astype(jnp.bfloat16),
        value_new,
        preferred_element_type=jnp.float32,
    )
    attended = (
        (summed / total[..., None]).astype(jnp.bfloat16).reshape(slot_count * DRAFT, query_cols)
    )
    wanted = slot_tokens
    picks = (tok_iota[:, None] == wanted[None, :]).astype(jnp.bfloat16)
    token_rows = jnp.dot(
        picks,
        lax.all_gather(attended, "feat", axis=0, tiled=True),
        preferred_element_type=jnp.float32,
    ).astype(jnp.bfloat16)
    outputs = jnp.dot(token_rows, output_weight, preferred_element_type=jnp.float32)
    return lax.psum_scatter(outputs.astype(jnp.bfloat16), "sub", scatter_dimension=0, tiled=True)


def solution(mesh):
    in_specs = (
        P("groups", "feat"),
        P("feat"),
        P("feat", "sub"),
        P("feat", "sub"),
        P("feat", "sub"),
        P("feat", None),
        P(None, "sub"),
        P("sub", "feat"),
        P("groups"),
        P("groups", None),
        P("groups"),
        P(("groups", "feat"), None, "sub"),
        P(("groups", "feat"), None, "sub"),
    )
    out_specs = P(("groups", "sub"), "feat")
    return jax.shard_map(body, mesh=mesh, in_specs=in_specs, out_specs=out_specs, check_vma=False)
```

profile of v0, /device:TPU:0, one launch (start us, length us, event | category | flops | bytes accessed | tf_op | source)
XLA Modules:
  0.0 105.6 jit_solution(8300614141563593867)
XLA Ops:
  6.5 0.0 copy-start
  6.5 0.0 reduce-scatter.2.cloned.1.call-start
  6.5 1.0 dynamic-slice_reduce_fusion
  7.6 0.2 convert_reduce_fusion
  7.7 0.1 fusion.43
  7.8 0.1 select_reduce_fusion.2
  7.9 0.7 convert_element_type.49
  8.6 1.0 fusion.19
  9.6 8.4 %psum.14 = f32[16]{0:T(128)S(1)} all-reduce(f32[16]{0:T(128)S(1)} %fusion.19), channel_id=1, replica_groups=mesh['groups'=2,'feat'=4,'sub'=4] {'feat'}, use_global_device_ids=true, to_apply=%region_5.6 | all-reduce | flops 16 | bytes 128 | tf_op jit(solution)/shard_map/psum | solution.py:56
  18.0 0.1 add_select_fusion
  18.0 0.1 select_n.89
  18.1 1.1 %convolution_convert_fusion = bf16[32,2048]{1,0:T(8,128)(2,1)S(1)} fusion(bf16[16,2048]{1,0:T(8,128)(2,1)} %param.13, f32[2048]{0:T(1024)S(1)} %convert_element_type.49, f32[16]{0:T(128)S(1)} %add_rsqrt_fusion, s32[32]{0:T(128)S(1)} %select_n.89), kind=kOutput, calls=%fused_computation.5 | convolution fusion | flops 2294272 | bytes 204992 | tf_op jit(solution)/shard_map/dot_general | solution.py:100
  19.2 1.2 %fusion.53 = f32[32,128]{1,0:T(8,128)S(1)} fusion(bf16[32,2048]{1,0:T(8,128)(2,1)S(1)} %convolution_convert_fusion, bf16[2048,128]{1,0:T(8,128)(2,1)} %param.17), kind=kOutput, calls=%fused_computation.92 | convolution fusion | flops 16777216 | bytes 671744 | tf_op jit(solution)/shard_map/dot_general | solution.py:108
  20.5 1.2 %fusion.52 = f32[32,128]{1,0:T(8,128)S(1)} fusion(bf16[32,2048]{1,0:T(8,128)(2,1)S(1)} %convolution_convert_fusion, bf16[2048,128]{1,0:T(8,128)(2,1)} %param.16), kind=kOutput, calls=%fused_computation.91 | convolution fusion | flops 16777216 | bytes 671744 | tf_op jit(solution)/shard_map/dot_general | solution.py:107
  21.7 0.0 copy-start.4
  21.7 0.0 copy-start.3
  21.7 3.1 %fusion.51 = f32[32,1024]{1,0:T(8,128)S(1)} fusion(bf16[32,2048]{1,0:T(8,128)(2,1)S(1)} %convolution_convert_fusion, bf16[2048,1024]{1,0:T(8,128)(2,1)} %param.15), kind=kOutput, calls=%fused_computation.90 | convolution fusion | flops 134217728 | bytes 4456448 | tf_op jit(solution)/shard_map/dot_general | solution.py:106
  24.8 0.0 copy-start.5
  24.8 0.0 copy-start.2
  24.8 0.7 pad_maximum_fusion
  25.5 0.0 reduce-scatter.2.cloned.1.call-update
  25.5 0.0 all-reduce.3.cloned.1.call-start
  25.6 0.0 copy-done.4
  25.6 0.1 broadcast_in_dim.146
  25.7 0.1 broadcast_in_dim.147
  25.7 0.0 copy-done
  25.7 0.0 copy-done.3
  25.7 0.4 convolution_select_fusion
  26.2 0.1 reshape.246
  26.3 5.9 %psum.15 = f32[16,64]{1,0:T(8,128)S(1)} all-reduce(f32[16,64]{1,0:T(8,128)S(1)} %reduce_sum.86), channel_id=1, replica_groups=mesh['groups'=2,'feat'=4,'sub'=4] {'feat'}, use_global_device_ids=true, to_apply=%region_9.10 | all-reduce | flops 1024 | bytes 8192 | tf_op jit(solution)/shard_map/psum | solution.py:96
  32.2 0.1 dynamic_slice.11
  32.2 0.2 fusion.35
  32.4 0.1 tile.5
  32.5 0.0 copy-done.5
  32.5 0.1 iota_add_fusion
  32.6 0.1 add.91
  32.7 0.2 select_reduce_fusion
  32.9 0.1 dynamic_slice.10
  32.9 0.2 fusion.46
  33.1 0.1 compare_select_fusion.2
  33.2 0.1 iota_compare_fusion
  33.3 0.1 compare_select_fusion
  33.4 12.2 %reduce-scatter.2.cloned.1.call-done = f32[8,1280]{1,0:T(8,128)} async-done(((f32[32,1280]{1,0:T(8,128)}), f32[8,1280]{1,0:T(8,128)}) %reduce-scatter.2.cloned.1.call-update) | async-done | bytes 40976 | tf_op jit(solution)/shard_map/reduce_scatter | solution.py:109
  45.6 0.9 subtract_convert_fusion.1
  46.5 0.0 copy-done.2
  46.5 1.3 %fusion.12 = f32[8,8,128]{2,0,1:T(8,128)S(1)} fusion(bf16[512,1024]{1,0:T(8,128)(2,1)S(1)} %copy-done.2, f32[8,1280]{1,0:T(8,128)} %reduce-scatter.2.cloned.1.call-done, f32[8,512]{1,0:T(8,128)S(1)} %tile.5, s32[512]{0:T(512)S(1)} %add_select_fusion.1, s32[8]{0:T(128)S(1)} %compare_select_fusion), kind=kOutput, calls=%fused_computation.14 | convolution fusion | flops 50348032 | bytes 1132576 | tf_op jit(solution)/shard_map/dot_general | solution.py:128
  47.8 0.1 subtract_convert_fusion
  47.9 0.1 pad_maximum_fusion.1
  48.0 0.0 copy-start.1
  48.0 3.9 %fusion.49 = (f32[2,4,8]{2,1,0:T(4,128)S(1)}, f32[2,4,8,8192]{3,2,1,0:T(8,128)S(1)}) fusion(bf16[2,4,8,128]{3,2,1,0:T(8,128)(2,1)S(1)} %bitcast.55, bf16[2,8192,128]{2,1,0:T(8,128)(2,1)} %param.24, pred[2,8192]{1,0:T(4,128)(4,1)S(1)} %iota_compare_fusion), kind=kOutput, calls=%fused_computation.88 | convolution fusion | flops 135790528 | bytes 6324480 | tf_op jit(solution)/shard_map/sdgx,scx->sdgc/dot_general | solution.py:154
  51.9 0.2 fusion.50
  52.2 0.7 slice.48
  52.9 0.2 fusion.28
  53.1 0.5 fusion.4
  53.5 0.0 copy-done.1
  53.5 0.8 fusion.13
  54.4 5.2 %all_gather.3 = bf16[32,1024]{1,0:T(8,128)(2,1)S(1)} all-gather(bf16[8,1024]{1,0:T(8,128)(2,1)S(1)} %bitcast.58), channel_id=1, replica_groups=mesh['groups'=2,'feat'=4,'sub'=4] {'feat'}, dimensions={0}, use_global_device_ids=true | all-gather | bytes 81920 | tf_op jit(solution)/shard_map/all_gather | solution.py:188
  59.6 0.0 copy-start.6
  59.6 3.6 %convolution_convert_fusion.1 = bf16[16,2048]{1,0:T(8,128)(2,1)} fusion(bf16[1024,2048]{1,0:T(8,128)(2,1)} %param.20, bf16[32,1024]{1,0:T(8,128)(2,1)S(1)} %all_gather.3, s32[32]{0:T(128)S(1)} %select_n.89), kind=kOutput, calls=%fused_computation.6 | convolution fusion | flops 68207104 | bytes 4325504 | tf_op jit(solution)/shard_map/dot_general | solution.py:191
  63.2 0.0 all-reduce.3.cloned.1.call-update
  63.2 0.0 copy-done.6
  63.2 0.6 dynamic-slice
  64.5 32.9 %all-reduce.3.cloned.1.call-done = bf16[16,2048]{1,0:T(8,128)(2,1)} async-done(((bf16[16,2048]{1,0:T(8,128)(2,1)}), bf16[16,2048]{1,0:T(8,128)(2,1)}) %all-reduce.3.cloned.1.call-update) | async-done | bytes 65552
  97.4 1.4 %constant_dynamic-slice_fusion = bf16[4,2048]{1,0:T(4,128)(2,1)} fusion(bf16[16,2048]{1,0:T(8,128)(2,1)} %all-reduce.3.cloned.1.call-done, u32[]{:T(128)S(6)} %multiply.13), kind=kLoop, calls=%fused_computation.79 | loop fusion | bytes 32772
  (15 shorter events, 0.1 us)
Async XLA Ops:
  6.5 19.2 %copy-start = (bf16[2048,512]{1,0:T(8,128)(2,1)S(1)}, bf16[2048,512]{1,0:T(8,128)(2,1)}, u32[]{:S(2)}) copy-start(bf16[2048,512]{1,0:T(8,128)(2,1)} %param.18) | copy-start | bytes 6291460
  6.5 39.1 %reduce-scatter.2.cloned.1.call-start = ((), (), s32[]{:S(2)}) async-start(), calls=%async_computation.1 | async-start | bytes 204800 | tf_op jit(solution)/shard_map/reduce_scatter | solution.py:109
  21.7 3.9 %copy-start.4 = (s32[4]{0:T(128)S(1)}, s32[4]{0:T(128)}, u32[]{:S(2)}) copy-start(s32[4]{0:T(128)} %param.21) | copy-start | bytes 52
  21.7 4.0 %copy-start.3 = (bf16[16,2048]{1,0:T(8,128)(2,1)S(1)}, bf16[16,2048]{1,0:T(8,128)(2,1)}, u32[]{:S(2)}) copy-start(bf16[16,2048]{1,0:T(8,128)(2,1)} %param.13) | copy-start | bytes 196612
  24.8 7.7 %copy-start.5 = (s32[4]{0:T(128)S(1)}, s32[4]{0:T(128)}, u32[]{:S(2)}) copy-start(s32[4]{0:T(128)} %param.23) | copy-start | bytes 52
  24.8 21.7 %copy-start.2 = (bf16[512,1024]{1,0:T(8,128)(2,1)S(1)}, bf16[512,1024]{1,0:T(8,128)(2,1)}, u32[]{:S(2)}) copy-start(bf16[512,1024]{1,0:T(8,128)(2,1)} %param.19) | copy-start | bytes 3145732
  25.5 71.9 %all-reduce.3.cloned.1.call-start = ((), (), s32[]{:S(2)}) async-start(), calls=%async_computation.2 | async-start | bytes 131072
  48.0 5.6 %copy-start.1 = (bf16[2,8192,128]{2,1,0:T(8,128)(2,1)S(1)}, bf16[2,8192,128]{2,1,0:T(8,128)(2,1)}, u32[]{:S(2)}) copy-start(bf16[2,8192,128]{2,1,0:T(8,128)(2,1)} %param.25) | copy-start | bytes 12582916
  59.6 3.6 %copy-start.6 = (u32[32]{0:T(128)S(1)}, u32[32]{0:T(128)}, u32[]{:S(2)}) copy-start(u32[32]{0:T(128)} %constant.68) | copy-start | bytes 388
Sparse Core Ops, SparseCore 0:
  25.6 19.9 reduce-scatter.1
  63.3 33.9 all-reduce.2
where the time goes:
time: 106 us
  waiting for transfers between devices  45.1 us (43%)
  blocking collectives  19.5 us (18%)
  matrix products  17.2 us (16%)
  between operations  14.3 us (13%)
  other arithmetic  5.08 us (5%)
  local copies, waits for them, and re-layouts  4.35 us (4%)
    unnamed x3, waiting for transfers between devices  32.9 us
    reduce_scatter x1, waiting for transfers between devices, body(): lax.psum_scatter(jnp.concatenate([query_part, key_part, value_part], axis...  12.2 us
    psum x1, blocking collectives, body(): squares = lax.psum(jnp.sum(hidden32 * hidden32, axis=1), 'feat')  8.37 us
    psum x1, blocking collectives, body(): adapter_token = lax.psum(adapter_token, 'feat')  5.86 us
    all_gather x1, blocking collectives, body(): lax.all_gather(attended, 'feat', axis=0, tiled=True)  5.25 us
    dot_general x1, matrix products, body(): jnp.einsum('sdgx,scx->sdgc', query, stored_keys, preferred_element_type=j...  3.9 us
    dot_general x1, matrix products, body(): jnp.dot(token_rows, output_weight, preferred_element_type=jnp.float32)  3.57 us
    dot_general x1, matrix products, body(): jnp.dot(rows_x, query_weight, preferred_element_type=jnp.float32)  3.05 us
  transfers between devices with their start and end apart: 2, of which 2 were waited for; matrix products, arithmetic and copies ran while one was open for 2% of the time, Pallas kernels for 0%

commit v1 on v0

v1 whole, which is shorter than its diff:
```python
import functools

import jax
import jax.numpy as jnp
import numpy as np
from jax import lax
from jax.experimental import pallas as pl
from jax.experimental.pallas import tpu as pltpu
from jax.sharding import PartitionSpec as P

ADAPTER_RANK = 64
DRAFT = 4
LANES = 128
SUB16 = 16

norm_eps = 1e-05
rope_base = 500000.0
LOG2E = 1.4426950408889634


def log2(n):
    assert n & (n - 1) == 0
    return n.bit_length() - 1


def wrap(value, n):
    return jnp.where(value >= n, value - n, value)


def kernel(
    feat,
    sub,
    chunk,
    adapter_ref,
    owner_ref,
    length_ref,
    hidden_hbm,
    gain_hbm,
    freq_hbm,
    wq_hbm,
    wk_hbm,
    wv_hbm,
    down_hbm,
    up_hbm,
    wo_hbm,
    keys_hbm,
    values_hbm,
    out_ref,
    hidden,
    gain,
    freq,
    wq,
    wk,
    wv,
    down,
    up,
    wo,
    keys,
    values,
    send_a,
    recv_a,
    send_q,
    recv_q,
    q_stage,
    scores,
    att_stage,
    att_all,
    out_stage,
    send_o,
    recv_o,
    load_sem,
    send_sem,
    recv_sem,
    att_send_sem,
    att_recv_sem,
    out_send_sem,
    out_recv_sem,
):
    f32, bf16, i32 = jnp.float32, jnp.bfloat16, jnp.int32
    me = lax.axis_index("feat")
    my_sub = lax.axis_index("sub")
    tokens, width = hidden.shape
    requests = tokens // DRAFT
    slots, context, head = keys.shape
    rows = slots * DRAFT
    query_cols = wq.shape[1]
    group = query_cols // head
    q_parts = send_q.shape[0]
    q_width = query_cols // q_parts
    lora_cols = down.shape[1]
    d_bits, r_bits, s_bits = log2(DRAFT), log2(rows), log2(slots)
    rank_bits = log2(ADAPTER_RANK)
    halves = SUB16 // rows
    half_cols = query_cols // halves
    out_rows = tokens // sub
    pieces = SUB16 // out_rows
    piece_cols = wo.shape[1] // pieces

    barrier = pltpu.get_barrier_semaphore()
    for o in range(1, feat):
        pl.semaphore_signal(
            barrier, inc=1, device_id={"feat": wrap(me + o, feat)},
            device_id_type=pl.DeviceIdType.MESH,
        )
    for o in range(1, sub):
        pl.semaphore_signal(
            barrier, inc=1, device_id={"sub": wrap(my_sub + o, sub)},
            device_id_type=pl.DeviceIdType.MESH,
        )

    loads = []

    def load(src, dst):
        copy = pltpu.make_async_copy(src, dst, load_sem.at[len(loads)])
        loads.append(copy)
        copy.start()
        return copy

    ld_hidden = load(hidden_hbm, hidden)
    ld_gain = load(gain_hbm, gain)
    ld_freq = load(freq_hbm, freq)
    ld_down = load(down_hbm, down)
    ld_wk = load(wk_hbm, wk)
    ld_wv = load(wv_hbm, wv)
    ld_q = [
        load(wq_hbm.at[:, pl.ds(i * q_width, q_width)], wq.at[:, pl.ds(i * q_width, q_width)])
        for i in range(q_parts)
    ]

    owner = [owner_ref[r, my_sub] for r in range(requests)]
    row_of = []
    for r in range(requests):
        slot = jnp.int32(0)
        for before in range(r):
            slot = slot + jnp.where(owner[before] == owner[r], 1, 0)
        row_of.append(owner[r] * slots + slot)
    adapter = [adapter_ref[r] for r in range(requests)]
    length = [length_ref[r] for r in range(requests)]
    my_adapter, my_length = [], []
    for k in range(slots):
        a, n = jnp.int32(-1), jnp.int32(0)
        for r in range(requests):
            here = row_of[r] == me * slots + k
            a = jnp.where(here, adapter[r], a)
            n = jnp.where(here, length[r], n)
        my_adapter.append(a)
        my_length.append(n)

    def iota(shape, dim):
        return lax.broadcasted_iota(i32, shape, dim)

    def per_request(index, scalars):
        out = jnp.full(index.shape, -1, i32)
        for r in range(requests):
            out = jnp.where(index == r, scalars[r], out)
        return out

    def target_row(j):
        return wrap(me + (j >> r_bits), feat) * slots + ((j >> d_bits) & (slots - 1))

    all_rows = feat * rows
    shape = (all_rows, tokens)
    j, t = iota(shape, 0), iota(shape, 1)
    picked = (per_request(t >> d_bits, row_of) == target_row(j)) & (
        (j & (DRAFT - 1)) == (t & (DRAFT - 1))
    )
    picks = jnp.where(picked, 1.0, 0.0).astype(bf16)

    shape = (all_rows, lora_cols)
    target = target_row(iota(shape, 0))
    row_adapter = jnp.full(shape, -1, i32)
    for r in range(requests):
        row_adapter = jnp.where(target == row_of[r], adapter[r], row_adapter)
    lora_mask = (iota(shape, 1) >> rank_bits) == row_adapter

    def slot_value(shape, scalars):
        index = iota(shape, 0) >> d_bits
        out = jnp.full(shape, scalars[0], i32)
        for k in range(1, slots):
            out = jnp.where(index == k, scalars[k], out)
        return out

    shape = (rows, lora_cols)
    my_lora_mask = (iota(shape, 1) >> rank_bits) == slot_value(shape, my_adapter)

    ld_hidden.wait()
    ld_gain.wait()
    ld_freq.wait()
    picked_hidden = jnp.dot(picks, hidden[...], preferred_element_type=f32)
    x = (picked_hidden * gain[...]).astype(bf16)
    squares = jnp.sum(picked_hidden * picked_hidden, axis=1, keepdims=True)

    shape = (rows, head)
    position = (slot_value(shape, my_length) + (iota(shape, 0) & (DRAFT - 1))).astype(f32)
    angle = position * freq[...]
    cosine = jnp.cos(angle)
    sine = jnp.sin(angle)
    sine = jnp.where(iota(shape, 1) < head // 2, -sine, sine)

    sends = []

    def send(src, dst, ssem, rsem, device):
        copy = pltpu.make_async_remote_copy(
            src_ref=src, dst_ref=dst, send_sem=ssem, recv_sem=rsem,
            device_id=device, device_id_type=pl.DeviceIdType.MESH,
        )
        copy.start()
        sends.append(copy)
        return copy

    ld_wk.wait()
    ld_wv.wait()
    ld_down.wait()
    ld_k = [load(keys_hbm.at[s], keys.at[s]) for s in range(slots)]
    ld_up = load(up_hbm, up)
    part_k = jnp.dot(x, wk[...], preferred_element_type=f32)
    part_v = jnp.dot(x, wv[...], preferred_element_type=f32)
    lora = jnp.where(lora_mask, jnp.dot(x, down[...], preferred_element_type=f32), 0.0)
    folded = lora[:, :LANES]
    for i in range(1, lora_cols // LANES):
        folded = folded + lora[:, i * LANES : (i + 1) * LANES]
    send_a[:, 0:head] = part_k
    send_a[:, head : 2 * head] = part_v
    send_a[:, 2 * head : 2 * head + LANES] = folded
    send_a[:, 2 * head + LANES :] = jnp.broadcast_to(squares, (all_rows, LANES))
    pl.semaphore_wait(barrier, feat + sub - 2)
    first = []
    for o in range(1, feat):
        block = pl.ds(o * rows, rows)
        first.append(
            send(
                send_a.at[block], recv_a.at[block], send_sem.at[0, o], recv_sem.at[0, o],
                {"feat": wrap(me + o, feat)},
            )
        )
    ld_v = []
    for i in range(q_parts):
        ld_q[i].wait()
        if i == 0:
            ld_v = [load(values_hbm.at[s], values.at[s]) for s in range(slots)]
        if i == q_parts - 1:
            ld_o = load(wo_hbm, wo)
        send_q[i] = jnp.dot(
            x, wq[:, i * q_width : (i + 1) * q_width], preferred_element_type=f32
        )
        for o in range(1, feat):
            block = pl.ds(o * rows, rows)
            first.append(
                send(
                    send_q.at[i, block], recv_q.at[i, block],
                    send_sem.at[1 + i, o], recv_sem.at[1 + i, o],
                    {"feat": wrap(me + o, feat)},
                )
            )
    ld_up.wait()
    for copy in first[: feat - 1]:
        copy.wait_recv()
    total_a = send_a[0:rows]
    for o in range(1, feat):
        total_a = total_a + recv_a[o * rows : (o + 1) * rows]
    scale = lax.rsqrt(total_a[:, 2 * head + LANES :] / (width * feat) + norm_eps)
    mid = total_a[:, 2 * head : 2 * head + LANES]
    mid = jnp.where(my_lora_mask, jnp.concatenate([mid] * (lora_cols // LANES), axis=1), 0.0)
    mid1 = mid.astype(bf16).astype(f32)
    rest = mid - mid1
    mid2 = rest.astype(bf16).astype(f32)
    mid3 = rest - mid2
    stacked = jnp.concatenate([mid1, mid2, mid3, jnp.zeros_like(mid)], axis=0).astype(bf16)
    lifted = jnp.dot(stacked, up[...], preferred_element_type=f32)
    lifted = lifted[0:rows] + lifted[rows : 2 * rows] + lifted[2 * rows : 3 * rows]

    def rotate(values_in):
        return values_in * cosine + pltpu.roll(values_in, head // 2, 1) * sine

    key_new = rotate(total_a[:, 0:head] * scale)
    value_new = total_a[:, head : 2 * head] * scale
    filler = jnp.zeros((LANES - rows, head), f32)
    key_new = jnp.concatenate([key_new, filler], axis=0).astype(bf16)
    value_new = jnp.concatenate([value_new, filler], axis=0).astype(bf16)

    for copy in first[feat - 1 :]:
        copy.wait_recv()
    for i in range(q_parts):
        total_q = send_q[i, 0:rows]
        for o in range(1, feat):
            total_q = total_q + recv_q[i, o * rows : (o + 1) * rows]
        for g in range(q_width // head):
            whole_g = i * (q_width // head) + g
            part = total_q[:, g * head : (g + 1) * head]
            part = part + lifted[:, whole_g * head : (whole_g + 1) * head]
            part = rotate(part * scale)
            for s in range(slots):
                q_stage[s, whole_g * DRAFT : (whole_g + 1) * DRAFT, :] = part[
                    s * DRAFT : (s + 1) * DRAFT
                ]

    for copy in ld_k + ld_v:
        copy.wait()
    factor = head ** (-0.5) * LOG2E
    q_rows = group * DRAFT
    chunks = context // chunk
    contract = (((1,), (1,)), ((), ()))
    shape = (q_rows, LANES)
    lane, row_d = iota(shape, 1), iota(shape, 0) & (DRAFT - 1)
    queries = [q_stage[s].astype(bf16) for s in range(slots)]
    new_scores, row_max = [], []
    for s in range(slots):
        fresh = lax.dot_general(queries[s], key_new, contract, preferred_element_type=f32)
        seen = (lane >= s * DRAFT) & (lane - s * DRAFT <= row_d)
        fresh = jnp.where(seen, fresh, -1e30)
        new_scores.append(fresh)
        top = fresh
        for c in range(chunks):
            block = lax.dot_general(
                queries[s], keys[s, c * chunk : (c + 1) * chunk, :], contract,
                preferred_element_type=f32,
            )
            valid = iota((q_rows, chunk), 1) < my_length[s] - c * chunk
            block = jnp.where(valid, block, -1e30)
            scores[s, :, c * chunk : (c + 1) * chunk] = block
            for i in range(chunk // LANES):
                top = jnp.maximum(top, block[:, i * LANES : (i + 1) * LANES])
        row_max.append(jnp.max(top, axis=1, keepdims=True))
    for s in range(slots):
        weights = jnp.exp2((new_scores[s] - row_max[s]) * factor)
        total = weights
        summed = jnp.dot(weights.astype(bf16), value_new, preferred_element_type=f32)
        for c in range(chunks):
            weights = jnp.exp2(
                (scores[s, :, c * chunk : (c + 1) * chunk] - row_max[s]) * factor
            )
            for i in range(chunk // LANES):
                total = total + weights[:, i * LANES : (i + 1) * LANES]
            summed = summed + jnp.dot(
                weights.astype(bf16), values[s, c * chunk : (c + 1) * chunk, :],
                preferred_element_type=f32,
            )
        attended = summed / jnp.sum(total, axis=1, keepdims=True)
        per_half = group // halves
        for g in range(group):
            h, at = g // per_half, g % per_half
            first_row = h * rows + s * DRAFT
            att_stage[first_row : first_row + DRAFT, at * head : (at + 1) * head] = attended[
                g * DRAFT : (g + 1) * DRAFT
            ]
    att_all[0:SUB16, :] = att_stage[...].astype(bf16)
    second = []
    for o in range(1, feat):
        second.append(
            send(
                att_all.at[pl.ds(0, SUB16)], att_all.at[pl.ds(o * SUB16, SUB16)],
                att_send_sem.at[o], att_recv_sem.at[o], {"feat": wrap(me + o, feat)},
            )
        )
    shape = (tokens, feat * SUB16)
    t, jj = iota(shape, 0), iota(shape, 1)
    out_bits = log2(out_rows)
    token = (wrap(my_sub + (t >> out_bits), sub) << out_bits) + (t & (out_rows - 1))
    source = me - (jj >> log2(SUB16))
    source = jnp.where(source < 0, source + feat, source)
    wanted = source * slots + ((jj >> d_bits) & (slots - 1))
    match = (per_request(token >> d_bits, row_of) == wanted) & (
        (token & (DRAFT - 1)) == (jj & (DRAFT - 1))
    )
    in_half = (jj & (SUB16 - 1)) >> r_bits
    ld_o.wait()
    for copy in second:
        copy.wait_recv()
    token_rows = jnp.concatenate(
        [
            jnp.dot(
                jnp.where(match & (in_half == h), 1.0, 0.0).astype(bf16), att_all[...],
                preferred_element_type=f32,
            )
            for h in range(halves)
        ],
        axis=1,
    ).astype(bf16)
    for p in range(pieces):
        block = jnp.dot(
            token_rows, wo[:, p * piece_cols : (p + 1) * piece_cols], preferred_element_type=f32
        )
        for o in range(sub):
            out_stage[o, p * out_rows : (p + 1) * out_rows, :] = block[
                o * out_rows : (o + 1) * out_rows
            ]
    third = []
    for o in range(1, sub):
        send_o[o] = out_stage[o].astype(bf16)
        third.append(
            send(
                send_o.at[o], recv_o.at[o], out_send_sem.at[o], out_recv_sem.at[o],
                {"sub": wrap(my_sub + o, sub)},
            )
        )
    for copy in third:
        copy.wait_recv()
    result = out_stage[0]
    for o in range(1, sub):
        result = result + recv_o[o].astype(f32)
    for p in range(pieces):
        out_ref[:, p * piece_cols : (p + 1) * piece_cols] = result[
            p * out_rows : (p + 1) * out_rows
        ].astype(bf16)
    for copy in sends:
        copy.wait_send()


def body(
    hidden,
    input_norm_gain,
    query_weight,
    key_weight,
    value_weight,
    adapter_down_weight,
    adapter_up_weight,
    output_weight,
    request_adapter,
    stored_owner,
    stored_lengths,
    stored_keys,
    stored_values,
):
    f32, bf16 = jnp.float32, jnp.bfloat16
    feat = lax.axis_size("feat")
    sub = lax.axis_size("sub")
    tokens, width = hidden.shape
    slots, context, head = stored_keys.shape
    rows = slots * DRAFT
    query_cols = query_weight.shape[1]
    out_cols = output_weight.shape[1]
    out_rows = tokens // sub
    q_parts = 2
    chunk = min(2048, context)
    pieces = SUB16 // out_rows
    half = head // 2
    inv_freq = (rope_base ** (-(np.arange(half) * 2.0) / head)).astype(np.float32)
    freq = jnp.asarray(np.tile(np.concatenate([inv_freq, inv_freq])[None, :], (rows, 1)))
    gain = input_norm_gain.astype(f32)[None, :]
    any_spec = pl.BlockSpec(memory_space=pl.ANY)
    smem = pl.BlockSpec(memory_space=pltpu.SMEM)
    V = pltpu.VMEM
    a_cols = 2 * head + 2 * LANES
    scratch = [
        V(hidden.shape, bf16),
        V(gain.shape, f32),
        V(freq.shape, f32),
        V(query_weight.shape, bf16),
        V(key_weight.shape, bf16),
        V(value_weight.shape, bf16),
        V(adapter_down_weight.shape, bf16),
        V(adapter_up_weight.shape, bf16),
        V(output_weight.shape, bf16),
        V(stored_keys.shape, bf16),
        V(stored_values.shape, bf16),
        V((feat * rows, a_cols), f32),
        V((feat * rows, a_cols), f32),
        V((q_parts, feat * rows, query_cols // q_parts), f32),
        V((q_parts, feat * rows, query_cols // q_parts), f32),
        V((slots, query_cols // head * DRAFT, head), f32),
        V((slots, query_cols // head * DRAFT, context), f32),
        V((SUB16, query_cols * rows // SUB16), f32),
        V((feat * SUB16, query_cols * rows // SUB16), bf16),
        V((sub, SUB16, out_cols // pieces), f32),
        V((sub, SUB16, out_cols // pieces), bf16),
        V((sub, SUB16, out_cols // pieces), bf16),
        pltpu.SemaphoreType.DMA((8 + q_parts + 2 * slots,)),
        pltpu.SemaphoreType.DMA((1 + q_parts, feat)),
        pltpu.SemaphoreType.DMA((1 + q_parts, feat)),
        pltpu.SemaphoreType.DMA((feat,)),
        pltpu.SemaphoreType.DMA((feat,)),
        pltpu.SemaphoreType.DMA((sub,)),
        pltpu.SemaphoreType.DMA((sub,)),
    ]
    return pl.pallas_call(
        functools.partial(kernel, feat, sub, chunk),
        out_shape=jax.ShapeDtypeStruct((out_rows, out_cols), bf16),
        in_specs=[smem] * 3 + [any_spec] * 11,
        out_specs=pl.BlockSpec(memory_space=pltpu.VMEM),
        scratch_shapes=scratch,
        compiler_params=pltpu.CompilerParams(
            collective_id=0, has_side_effects=True, vmem_limit_bytes=48 * 1024 * 1024
        ),
    )(
        request_adapter,
        stored_owner,
        stored_lengths,
        hidden,
        gain,
        freq,
        query_weight,
        key_weight,
        value_weight,
        adapter_down_weight,
        adapter_up_weight,
        output_weight,
        stored_keys,
        stored_values,
    )


def solution(mesh):
    in_specs = (
        P("groups", "feat"),
        P("feat"),
        P("feat", "sub"),
        P("feat", "sub"),
        P("feat", "sub"),
        P("feat", None),
        P(None, "sub"),
        P("sub", "feat"),
        P("groups"),
        P("groups", None),
        P("groups"),
        P(("groups", "feat"), None, "sub"),
        P(("groups", "feat"), None, "sub"),
    )
    out_specs = P(("groups", "sub"), "feat")
    return jax.shard_map(body, mesh=mesh, in_specs=in_specs, out_specs=out_specs, check_vma=False)
```

time: 106 us -> 29.5 us (0.28)
  waiting for transfers between devices: 45.1 us -> 0 us
  blocking collectives: 19.5 us -> 0 us
  Pallas kernels: 0 us -> 19.4 us
  matrix products: 17.2 us -> 0 us
  between operations: 14.3 us -> 0.02 us
  local copies, waits for them, and re-layouts: 4.35 us -> 9.02 us
  other arithmetic: 5.08 us -> 0.69 us
    unnamed x3 -> x0, waiting for transfers between devices: 32.9 us -> none
    pallas_call x0 -> x1, Pallas kernels: none -> 19.4 us  [body(): pl.pallas_call(functools.partial(kernel, feat, sub, chunk), out_shape=jax...]
    dot_general x12 -> x0, matrix products: 17.2 us -> none  [the longest x1 3.9 us: body(): jnp.einsum('sdgx,scx->sdgc', query, stored_keys, preferred_element_type=j...]
    psum x2 -> x0, blocking collectives: 14.2 us -> none  [the longest x1 8.37 us: body(): squares = lax.psum(jnp.sum(hidden32 * hidden32, axis=1), 'feat')]
    reduce_scatter x1 -> x0, waiting for transfers between devices: 12.2 us -> none  [body(): lax.psum_scatter(jnp.concatenate([query_part, key_part, value_part], axis...]
    unnamed x17 -> x19, local copies, waits for them, and re-layouts: 2 us -> 9.02 us
    all_gather x1 -> x0, blocking collectives: 5.25 us -> none  [body(): lax.all_gather(attended, 'feat', axis=0, tiled=True)]
    reduce_sum x8 -> x0, other arithmetic: 2.13 us -> none  [the longest x1 0.97 us: body(): squares = lax.psum(jnp.sum(hidden32 * hidden32, axis=1), 'feat')]
  transfers between devices with their start and end apart: 2 -> 0, of which waited for: 2 -> 0; matrix products, arithmetic and copies ran while one was open for 2% -> 0% of each run, Pallas kernels for 0% -> 0%
where the time goes in v1:
time: 29.5 us; the launch traced here: 29.1 us
  Pallas kernels  19.4 us (66%)
  local copies, waits for them, and re-layouts  9.02 us (31%)
  other arithmetic  0.69 us (2%)
    pallas_call x1, Pallas kernels, body(): pl.pallas_call(functools.partial(kernel, feat, sub, chunk), out_shape=jax...  19.4 us
    unnamed x19, local copies, waits for them, and re-layouts  9.02 us
    broadcast_in_dim x1, other arithmetic, body(): gain = input_norm_gain.astype(f32)[None, :]  0.69 us

profile of v1, /device:TPU:0, one launch (start us, length us, event | category | flops | bytes accessed | tf_op | source)
XLA Modules:
  0.0 29.1 jit_solution(6371298246364379613)
XLA Ops:
  0.0 0.7 %broadcast_in_dim.7 = f32[2048]{0:T(1024)S(1)} convert(bf16[2048]{0:T(1024)(128)(2,1)} %param.15) | non-fusion elementwise | flops 2048 | bytes 12288 | tf_op jit(solution)/shard_map/broadcast_in_dim | solution.py:439
  0.7 0.0 copy-start
  0.7 1.6 %copy-done = bf16[2048,512]{1,0:T(8,128)(2,1)S(1)} copy-done((bf16[2048,512]{1,0:T(8,128)(2,1)S(1)}, bf16[2048,512]{1,0:T(8,128)(2,1)}, u32[]{:S(2)}) %copy-start) | copy-done | bytes 2097176
  2.3 0.0 copy-start.1
  2.3 1.2 %copy-done.1 = bf16[512,1024]{1,0:T(8,128)(2,1)S(1)} copy-done((bf16[512,1024]{1,0:T(8,128)(2,1)S(1)}, bf16[512,1024]{1,0:T(8,128)(2,1)}, u32[]{:S(2)}) %copy-start.1) | copy-done | bytes 1048600
  3.5 0.0 copy-start.2
  3.5 1.0 %copy-done.2 = bf16[2048,128]{1,0:T(8,128)(2,1)S(1)} copy-done((bf16[2048,128]{1,0:T(8,128)(2,1)S(1)}, bf16[2048,128]{1,0:T(8,128)(2,1)}, u32[]{:S(2)}) %copy-start.2) | copy-done | bytes 524312
  4.5 0.0 copy-start.3
  4.6 1.0 %copy-done.3 = bf16[2048,128]{1,0:T(8,128)(2,1)S(1)} copy-done((bf16[2048,128]{1,0:T(8,128)(2,1)S(1)}, bf16[2048,128]{1,0:T(8,128)(2,1)}, u32[]{:S(2)}) %copy-start.3) | copy-done | bytes 524312
  5.6 0.0 copy-start.4
  5.6 0.8 %copy-done.4 = bf16[16,2048]{1,0:T(8,128)(2,1)S(1)} copy-done((bf16[16,2048]{1,0:T(8,128)(2,1)S(1)}, bf16[16,2048]{1,0:T(8,128)(2,1)}, u32[]{:S(2)}) %copy-start.4) | copy-done | bytes 65560
  6.4 0.0 copy-start.5
  6.4 0.7 %copy-done.5 = f32[8,128]{1,0:T(8,128)S(1)} copy-done((f32[8,128]{1,0:T(8,128)S(1)}, f32[8,128]{1,0:T(8,128)}, u32[]{:S(2)}) %copy-start.5) | copy-done | bytes 4120
  7.1 0.0 copy-start.6
  7.1 0.7 %copy-done.6 = s32[4,4]{1,0:T(4,128)S(1)} copy-done((s32[4,4]{1,0:T(4,128)S(1)}, s32[4,4]{1,0:T(4,128)}, u32[]{:S(2)}) %copy-start.6) | copy-done | bytes 88
  7.8 0.0 copy-start.7
  7.8 0.7 %copy-done.7 = s32[4]{0:T(128)S(1)} copy-done((s32[4]{0:T(128)S(1)}, s32[4]{0:T(128)}, u32[]{:S(2)}) %copy-start.7) | copy-done | bytes 40
  8.5 0.0 copy-start.8
  8.5 0.7 %copy-done.8 = s32[4]{0:T(128)S(1)} copy-done((s32[4]{0:T(128)S(1)}, s32[4]{0:T(128)}, u32[]{:S(2)}) %copy-start.8) | copy-done | bytes 40
  9.1 19.4 %shard_map.136 = bf16[4,2048]{1,0:T(4,128)(2,1)S(1)} custom-call(s32[4]{0:T(128)S(1)} %copy-done.7, s32[4,4]{1,0:T(4,128)S(1)} %copy-done.6, s32[4]{0:T(128)S(1)} %copy-done.8, bf16[16,2048]{1,0:T(8,128)(2,1)S(1)} %copy-done.4, f32[1,2048]{1,0:T(1,128)S(1)} %bitcast.1, f32[8,128]{1,0:T(8,128)S(1)} %copy-done.5, bf16[2048,1024]{1,0:T(8,128)(2,1)} %wq_hbm.1, ...), custom_call_target="tpu_custom_call" | custom-call | tf_op jit(solution)/shard_map/pallas_call | solution.py:475
  28.5 0.6 %copy.16 = bf16[4,2048]{1,0:T(4,128)(2,1)} copy(bf16[4,2048]{1,0:T(4,128)(2,1)S(1)} %shard_map.136) | data formatting | bytes 32768
Async XLA Ops:
  0.7 1.6 %copy-start = (bf16[2048,512]{1,0:T(8,128)(2,1)S(1)}, bf16[2048,512]{1,0:T(8,128)(2,1)}, u32[]{:S(2)}) copy-start(bf16[2048,512]{1,0:T(8,128)(2,1)} %down_hbm.1) | copy-start | bytes 6291460
  2.3 1.2 %copy-start.1 = (bf16[512,1024]{1,0:T(8,128)(2,1)S(1)}, bf16[512,1024]{1,0:T(8,128)(2,1)}, u32[]{:S(2)}) copy-start(bf16[512,1024]{1,0:T(8,128)(2,1)} %up_hbm.1) | copy-start | bytes 3145732
  3.5 1.0 %copy-start.2 = (bf16[2048,128]{1,0:T(8,128)(2,1)S(1)}, bf16[2048,128]{1,0:T(8,128)(2,1)}, u32[]{:S(2)}) copy-start(bf16[2048,128]{1,0:T(8,128)(2,1)} %wk_hbm.1) | copy-start | bytes 1572868
  4.5 1.0 %copy-start.3 = (bf16[2048,128]{1,0:T(8,128)(2,1)S(1)}, bf16[2048,128]{1,0:T(8,128)(2,1)}, u32[]{:S(2)}) copy-start(bf16[2048,128]{1,0:T(8,128)(2,1)} %wv_hbm.1) | copy-start | bytes 1572868
  5.6 0.8 %copy-start.4 = (bf16[16,2048]{1,0:T(8,128)(2,1)S(1)}, bf16[16,2048]{1,0:T(8,128)(2,1)}, u32[]{:S(2)}) copy-start(bf16[16,2048]{1,0:T(8,128)(2,1)} %hidden_hbm.1) | copy-start | bytes 196612
  6.4 0.7 %copy-start.5 = (f32[8,128]{1,0:T(8,128)S(1)}, f32[8,128]{1,0:T(8,128)}, u32[]{:S(2)}) copy-start(f32[8,128]{1,0:T(8,128)} %constant.2.clone.freq_hbm) | copy-start | bytes 12292
  7.1 0.7 %copy-start.6 = (s32[4,4]{1,0:T(4,128)S(1)}, s32[4,4]{1,0:T(4,128)}, u32[]{:S(2)}) copy-start(s32[4,4]{1,0:T(4,128)} %owner_ref.1) | copy-start | bytes 196
  7.8 0.7 %copy-start.7 = (s32[4]{0:T(128)S(1)}, s32[4]{0:T(128)}, u32[]{:S(2)}) copy-start(s32[4]{0:T(128)} %adapter_ref.1) | copy-start | bytes 52
  8.5 0.7 %copy-start.8 = (s32[4]{0:T(128)S(1)}, s32[4]{0:T(128)}, u32[]{:S(2)}) copy-start(s32[4]{0:T(128)} %length_ref.1) | copy-start | bytes 52

commit v2 on v1

--- a/solution.py
+++ b/solution.py
@@ -31,9 +31,9 @@
     feat,
     sub,
     chunk,
-    adapter_ref,
-    owner_ref,
-    length_ref,
+    adapter_hbm,
+    owner_hbm,
+    length_hbm,
     hidden_hbm,
     gain_hbm,
     freq_hbm,
@@ -46,6 +46,9 @@
     keys_hbm,
     values_hbm,
     out_ref,
+    adapter_ref,
+    owner_ref,
+    length_ref,
     hidden,
     gain,
     freq,
@@ -116,6 +119,9 @@
         copy.start()
         return copy
 
+    ld_index = [
+        load(owner_hbm, owner_ref), load(adapter_hbm, adapter_ref), load(length_hbm, length_ref)
+    ]
     ld_hidden = load(hidden_hbm, hidden)
     ld_gain = load(gain_hbm, gain)
     ld_freq = load(freq_hbm, freq)
@@ -127,6 +133,8 @@
         for i in range(q_parts)
     ]
 
+    for copy in ld_index:
+        copy.wait()
     owner = [owner_ref[r, my_sub] for r in range(requests)]
     row_of = []
     for r in range(requests):
@@ -187,7 +195,14 @@
     ld_gain.wait()
     ld_freq.wait()
     picked_hidden = jnp.dot(picks, hidden[...], preferred_element_type=f32)
-    x = (picked_hidden * gain[...]).astype(bf16)
+    gains = gain[...].astype(f32)
+    x = jnp.concatenate(
+        [
+            picked_hidden[:, i * LANES : (i + 1) * LANES] * gains[i : i + 1, :]
+            for i in range(width // LANES)
+        ],
+        axis=1,
+    ).astype(bf16)
     squares = jnp.sum(picked_hidden * picked_hidden, axis=1, keepdims=True)
 
     shape = (rows, head)
@@ -436,14 +451,16 @@
     half = head // 2
     inv_freq = (rope_base ** (-(np.arange(half) * 2.0) / head)).astype(np.float32)
     freq = jnp.asarray(np.tile(np.concatenate([inv_freq, inv_freq])[None, :], (rows, 1)))
-    gain = input_norm_gain.astype(f32)[None, :]
+    gain = input_norm_gain.reshape(-1, LANES)
     any_spec = pl.BlockSpec(memory_space=pl.ANY)
-    smem = pl.BlockSpec(memory_space=pltpu.SMEM)
     V = pltpu.VMEM
     a_cols = 2 * head + 2 * LANES
     scratch = [
+        pltpu.SMEM(request_adapter.shape, jnp.int32),
+        pltpu.SMEM(stored_owner.shape, jnp.int32),
+        pltpu.SMEM(stored_lengths.shape, jnp.int32),
         V(hidden.shape, bf16),
-        V(gain.shape, f32),
+        V(gain.shape, bf16),
         V(freq.shape, f32),
         V(query_weight.shape, bf16),
         V(key_weight.shape, bf16),
@@ -464,7 +481,7 @@
         V((sub, SUB16, out_cols // pieces), f32),
         V((sub, SUB16, out_cols // pieces), bf16),
         V((sub, SUB16, out_cols // pieces), bf16),
-        pltpu.SemaphoreType.DMA((8 + q_parts + 2 * slots,)),
+        pltpu.SemaphoreType.DMA((11 + q_parts + 2 * slots,)),
         pltpu.SemaphoreType.DMA((1 + q_parts, feat)),
         pltpu.SemaphoreType.DMA((1 + q_parts, feat)),
         pltpu.SemaphoreType.DMA((feat,)),
@@ -475,11 +492,11 @@
     return pl.pallas_call(
         functools.partial(kernel, feat, sub, chunk),
         out_shape=jax.ShapeDtypeStruct((out_rows, out_cols), bf16),
-        in_specs=[smem] * 3 + [any_spec] * 11,
+        in_specs=[any_spec] * 14,
         out_specs=pl.BlockSpec(memory_space=pltpu.VMEM),
         scratch_shapes=scratch,
         compiler_params=pltpu.CompilerParams(
-            collective_id=0, has_side_effects=True, vmem_limit_bytes=48 * 1024 * 1024
+            collective_id=0, has_side_effects=True, vmem_limit_bytes=64 * 1024 * 1024
         ),
     )(
         request_adapter,

time: 29.5 us -> 21.7 us (0.74)
  local copies, waits for them, and re-layouts: 9.02 us -> 1.33 us
  Pallas kernels: 19.4 us -> 20.1 us
  other arithmetic: 0.69 us -> 0 us
    unnamed x19 -> x1, local copies, waits for them, and re-layouts: 9.02 us -> 1.33 us
    pallas_call x1, Pallas kernels: 19.4 us -> 20.1 us  [body(): pl.pallas_call(functools.partial(kernel, feat, sub, chunk), out_shape=jax...]
    broadcast_in_dim x1 -> x0, other arithmetic: 0.69 us -> none  [body(): gain = input_norm_gain.astype(f32)[None, :]]
where the time goes in v2:
time: 21.7 us; the launch traced here: 21.5 us
  Pallas kernels  20.1 us (93%)
  local copies, waits for them, and re-layouts  1.33 us (6%)
    pallas_call x1, Pallas kernels, body(): pl.pallas_call(functools.partial(kernel, feat, sub, chunk), out_shape=jax...  20.1 us
    unnamed x1, local copies, waits for them, and re-layouts  1.33 us

profile of v2, /device:TPU:0, one launch (start us, length us, event | category | flops | bytes accessed | tf_op | source)
XLA Modules:
  0.0 21.5 jit_solution(4539191785453780579)
XLA Ops:
  0.0 20.1 %shard_map.136 = bf16[4,2048]{1,0:T(4,128)(2,1)} custom-call(s32[4]{0:T(128)} %adapter_hbm.1, s32[4,4]{1,0:T(4,128)} %owner_hbm.1, s32[4]{0:T(128)} %length_hbm.1, bf16[16,2048]{1,0:T(8,128)(2,1)} %hidden_hbm.1, bf16[16,128]{1,0:T(8,128)(2,1)} %bitcast.1, f32[8,128]{1,0:T(8,128)} %constant.2.clone.freq_hbm, bf16[2048,1024]{1,0:T(8,128)(2,1)} %wq_hbm.1, ...), custom_call_target="tpu_custom_call" | custom-call | tf_op jit(solution)/shard_map/pallas_call | solution.py:492
  20.2 1.3 %copy.16 = bf16[4,2048]{1,0:T(4,128)(2,1)} copy(bf16[4,2048]{1,0:T(4,128)(2,1)} %shard_map.136) | data formatting | bytes 32768

commit v3 on v2

--- a/solution.py
+++ b/solution.py
@@ -84,7 +84,7 @@
     my_sub = lax.axis_index("sub")
     tokens, width = hidden.shape
     requests = tokens // DRAFT
-    slots, context, head = keys.shape
+    slots, context, head = keys_hbm.shape
     rows = slots * DRAFT
     query_cols = wq.shape[1]
     group = query_cols // head
@@ -94,10 +94,12 @@
     d_bits, r_bits, s_bits = log2(DRAFT), log2(rows), log2(slots)
     rank_bits = log2(ADAPTER_RANK)
     halves = SUB16 // rows
-    half_cols = query_cols // halves
+    q_rows = group * DRAFT
     out_rows = tokens // sub
     pieces = SUB16 // out_rows
-    piece_cols = wo.shape[1] // pieces
+    o_parts = send_o.shape[0]
+    part_cols = wo.shape[1] // o_parts
+    piece_cols = part_cols // pieces
 
     barrier = pltpu.get_barrier_semaphore()
     for o in range(1, feat):
@@ -191,6 +193,7 @@
     shape = (rows, lora_cols)
     my_lora_mask = (iota(shape, 1) >> rank_bits) == slot_value(shape, my_adapter)
 
+    q_stage[...] = jnp.zeros_like(q_stage)
     ld_hidden.wait()
     ld_gain.wait()
     ld_freq.wait()
@@ -226,7 +229,9 @@
     ld_wk.wait()
     ld_wv.wait()
     ld_down.wait()
-    ld_k = [load(keys_hbm.at[s], keys.at[s]) for s in range(slots)]
+    ld_k = [
+        load(keys_hbm.at[s], keys.at[:, pl.ds(s * head, head)]) for s in range(slots)
+    ]
     ld_up = load(up_hbm, up)
     part_k = jnp.dot(x, wk[...], preferred_element_type=f32)
     part_v = jnp.dot(x, wv[...], preferred_element_type=f32)
@@ -252,9 +257,18 @@
     for i in range(q_parts):
         ld_q[i].wait()
         if i == 0:
-            ld_v = [load(values_hbm.at[s], values.at[s]) for s in range(slots)]
+            ld_v = [
+                load(values_hbm.at[s], values.at[:, pl.ds(s * head, head)])
+                for s in range(slots)
+            ]
         if i == q_parts - 1:
-            ld_o = load(wo_hbm, wo)
+            ld_o = [
+                load(
+                    wo_hbm.at[:, pl.ds(n * part_cols, part_cols)],
+                    wo.at[:, pl.ds(n * part_cols, part_cols)],
+                )
+                for n in range(o_parts)
+            ]
         send_q[i] = jnp.dot(
             x, wq[:, i * q_width : (i + 1) * q_width], preferred_element_type=f32
         )
@@ -305,52 +319,60 @@
             part = part + lifted[:, whole_g * head : (whole_g + 1) * head]
             part = rotate(part * scale)
             for s in range(slots):
-                q_stage[s, whole_g * DRAFT : (whole_g + 1) * DRAFT, :] = part[
+                at_row = s * q_rows + whole_g * DRAFT
+                q_stage[at_row : at_row + DRAFT, s * head : (s + 1) * head] = part[
                     s * DRAFT : (s + 1) * DRAFT
                 ]
 
     for copy in ld_k + ld_v:
         copy.wait()
     factor = head ** (-0.5) * LOG2E
-    q_rows = group * DRAFT
     chunks = context // chunk
     contract = (((1,), (1,)), ((), ()))
-    shape = (q_rows, LANES)
-    lane, row_d = iota(shape, 1), iota(shape, 0) & (DRAFT - 1)
-    queries = [q_stage[s].astype(bf16) for s in range(slots)]
-    new_scores, row_max = [], []
+    queries = q_stage[...]
+    flat = queries[:, 0:head]
+    for k in range(1, slots):
+        flat = flat + queries[:, k * head : (k + 1) * head]
+    queries = queries.astype(bf16)
+
+    def row_slot(shape):
+        return iota(shape, 0) >> log2(q_rows)
+
+    shape = (slots * q_rows, LANES)
+    draft = iota(shape, 1) - row_slot(shape) * DRAFT
+    fresh = lax.dot_general(flat.astype(bf16), key_new, contract, preferred_element_type=f32)
+    fresh = jnp.where((draft >= 0) & (draft <= (iota(shape, 0) & (DRAFT - 1))), fresh, -1e30)
+    shape = (slots * q_rows, chunk)
+    limit = jnp.full(shape, my_length[0], i32)
+    for k in range(1, slots):
+        limit = jnp.where(row_slot(shape) == k, my_length[k], limit)
+    top = fresh
+    for c in range(chunks):
+        block = lax.dot_general(
+            queries, keys[c * chunk : (c + 1) * chunk, :], contract, preferred_element_type=f32
+        )
+        block = jnp.where(iota(shape, 1) + c * chunk < limit, block, -1e30)
+        scores[:, c * chunk : (c + 1) * chunk] = block
+        for i in range(chunk // LANES):
+            top = jnp.maximum(top, block[:, i * LANES : (i + 1) * LANES])
+    row_max = jnp.max(top, axis=1, keepdims=True)
+    weights = jnp.exp2((fresh - row_max) * factor)
+    total = weights
+    summed_new = jnp.dot(weights.astype(bf16), value_new, preferred_element_type=f32)
+    summed = jnp.zeros((slots * q_rows, slots * head), f32)
+    for c in range(chunks):
+        weights = jnp.exp2((scores[:, c * chunk : (c + 1) * chunk] - row_max) * factor)
+        for i in range(chunk // LANES):
+            total = total + weights[:, i * LANES : (i + 1) * LANES]
+        summed = summed + jnp.dot(
+            weights.astype(bf16), values[c * chunk : (c + 1) * chunk, :],
+            preferred_element_type=f32,
+        )
+    denominator = jnp.sum(total, axis=1, keepdims=True)
     for s in range(slots):
-        fresh = lax.dot_general(queries[s], key_new, contract, preferred_element_type=f32)
-        seen = (lane >= s * DRAFT) & (lane - s * DRAFT <= row_d)
-        fresh = jnp.where(seen, fresh, -1e30)
-        new_scores.append(fresh)
-        top = fresh
-        for c in range(chunks):
-            block = lax.dot_general(
-                queries[s], keys[s, c * chunk : (c + 1) * chunk, :], contract,
-                preferred_element_type=f32,
-            )
-            valid = iota((q_rows, chunk), 1) < my_length[s] - c * chunk
-            block = jnp.where(valid, block, -1e30)
-            scores[s, :, c * chunk : (c + 1) * chunk] = block
-            for i in range(chunk // LANES):
-                top = jnp.maximum(top, block[:, i * LANES : (i + 1) * LANES])
-        row_max.append(jnp.max(top, axis=1, keepdims=True))
-    for s in range(slots):
-        weights = jnp.exp2((new_scores[s] - row_max[s]) * factor)
-        total = weights
-        summed = jnp.dot(weights.astype(bf16), value_new, preferred_element_type=f32)
-        for c in range(chunks):
-            weights = jnp.exp2(
-                (scores[s, :, c * chunk : (c + 1) * chunk] - row_max[s]) * factor
-            )
-            for i in range(chunk // LANES):
-                total = total + weights[:, i * LANES : (i + 1) * LANES]
-            summed = summed + jnp.dot(
-                weights.astype(bf16), values[s, c * chunk : (c + 1) * chunk, :],
-                preferred_element_type=f32,
-            )
-        attended = summed / jnp.sum(total, axis=1, keepdims=True)
+        span = slice(s * q_rows, (s + 1) * q_rows)
+        attended = summed[span, s * head : (s + 1) * head] + summed_new[span]
+        attended = attended / denominator[span]
         per_half = group // halves
         for g in range(group):
             h, at = g // per_half, g % per_half
@@ -378,7 +400,6 @@
         (token & (DRAFT - 1)) == (jj & (DRAFT - 1))
     )
     in_half = (jj & (SUB16 - 1)) >> r_bits
-    ld_o.wait()
     for copy in second:
         copy.wait_recv()
     token_rows = jnp.concatenate(
@@ -391,32 +412,36 @@
         ],
         axis=1,
     ).astype(bf16)
-    for p in range(pieces):
+    third = []
+    for n in range(o_parts):
+        ld_o[n].wait()
         block = jnp.dot(
-            token_rows, wo[:, p * piece_cols : (p + 1) * piece_cols], preferred_element_type=f32
-        )
-        for o in range(sub):
-            out_stage[o, p * out_rows : (p + 1) * out_rows, :] = block[
-                o * out_rows : (o + 1) * out_rows
-            ]
-    third = []
-    for o in range(1, sub):
-        send_o[o] = out_stage[o].astype(bf16)
-        third.append(
-            send(
-                send_o.at[o], recv_o.at[o], out_send_sem.at[o], out_recv_sem.at[o],
-                {"sub": wrap(my_sub + o, sub)},
+            token_rows, wo[:, n * part_cols : (n + 1) * part_cols], preferred_element_type=f32
+        )
+        for p in range(pieces):
+            for o in range(sub):
+                out_stage[n, o, p * out_rows : (p + 1) * out_rows, :] = block[
+                    o * out_rows : (o + 1) * out_rows, p * piece_cols : (p + 1) * piece_cols
+                ]
+        for o in range(1, sub):
+            send_o[n, o] = out_stage[n, o].astype(bf16)
+            third.append(
+                send(
+                    send_o.at[n, o], recv_o.at[n, o], out_send_sem.at[n, o],
+                    out_recv_sem.at[n, o], {"sub": wrap(my_sub + o, sub)},
+                )
             )
-        )
     for copy in third:
         copy.wait_recv()
-    result = out_stage[0]
-    for o in range(1, sub):
-        result = result + recv_o[o].astype(f32)
-    for p in range(pieces):
-        out_ref[:, p * piece_cols : (p + 1) * piece_cols] = result[
-            p * out_rows : (p + 1) * out_rows
-        ].astype(bf16)
+    for n in range(o_parts):
+        result = out_stage[n, 0]
+        for o in range(1, sub):
+            result = result + recv_o[n, o].astype(f32)
+        for p in range(pieces):
+            first_col = n * part_cols + p * piece_cols
+            out_ref[:, first_col : first_col + piece_cols] = result[
+                p * out_rows : (p + 1) * out_rows
+            ].astype(bf16)
     for copy in sends:
         copy.wait_send()
 
@@ -446,6 +471,7 @@
     out_cols = output_weight.shape[1]
     out_rows = tokens // sub
     q_parts = 2
+    o_parts = 2
     chunk = min(2048, context)
     pieces = SUB16 // out_rows
     half = head // 2
@@ -468,35 +494,35 @@
         V(adapter_down_weight.shape, bf16),
         V(adapter_up_weight.shape, bf16),
         V(output_weight.shape, bf16),
-        V(stored_keys.shape, bf16),
-        V(stored_values.shape, bf16),
+        V((context, slots * head), bf16),
+        V((context, slots * head), bf16),
         V((feat * rows, a_cols), f32),
         V((feat * rows, a_cols), f32),
         V((q_parts, feat * rows, query_cols // q_parts), f32),
         V((q_parts, feat * rows, query_cols // q_parts), f32),
-        V((slots, query_cols // head * DRAFT, head), f32),
-        V((slots, query_cols // head * DRAFT, context), f32),
+        V((slots * query_cols // head * DRAFT, slots * head), f32),
+        V((slots * query_cols // head * DRAFT, context), f32),
         V((SUB16, query_cols * rows // SUB16), f32),
         V((feat * SUB16, query_cols * rows // SUB16), bf16),
-        V((sub, SUB16, out_cols // pieces), f32),
-        V((sub, SUB16, out_cols // pieces), bf16),
-        V((sub, SUB16, out_cols // pieces), bf16),
-        pltpu.SemaphoreType.DMA((11 + q_parts + 2 * slots,)),
+        V((o_parts, sub, SUB16, out_cols // pieces // o_parts), f32),
+        V((o_parts, sub, SUB16, out_cols // pieces // o_parts), bf16),
+        V((o_parts, sub, SUB16, out_cols // pieces // o_parts), bf16),
+        pltpu.SemaphoreType.DMA((11 + o_parts + q_parts + 2 * slots,)),
         pltpu.SemaphoreType.DMA((1 + q_parts, feat)),
         pltpu.SemaphoreType.DMA((1 + q_parts, feat)),
         pltpu.SemaphoreType.DMA((feat,)),
         pltpu.SemaphoreType.DMA((feat,)),
-        pltpu.SemaphoreType.DMA((sub,)),
-        pltpu.SemaphoreType.DMA((sub,)),
+        pltpu.SemaphoreType.DMA((o_parts, sub)),
+        pltpu.SemaphoreType.DMA((o_parts, sub)),
     ]
     return pl.pallas_call(
         functools.partial(kernel, feat, sub, chunk),
-        out_shape=jax.ShapeDtypeStruct((out_rows, out_cols), bf16),
+        out_shape=pltpu.VMEM((out_rows, out_cols), bf16),
         in_specs=[any_spec] * 14,
         out_specs=pl.BlockSpec(memory_space=pltpu.VMEM),
         scratch_shapes=scratch,
         compiler_params=pltpu.CompilerParams(
-            collective_id=0, has_side_effects=True, vmem_limit_bytes=64 * 1024 * 1024
+            collective_id=0, has_side_effects=True, vmem_limit_bytes=63 * 1024 * 1024
         ),
     )(
         request_adapter,

time: 21.7 us -> 21.9 us (level)
  Pallas kernels: 20.1 us -> 21.1 us
  local copies, waits for them, and re-layouts: 1.33 us -> 0.61 us
    pallas_call x1, Pallas kernels: 20.1 us -> 21.1 us  [body(): pl.pallas_call(functools.partial(kernel, feat, sub, chunk), out_shape=plt...]
    unnamed x1, local copies, waits for them, and re-layouts: 1.33 us -> 0.61 us
where the time goes in v3:
time: 21.9 us; the launch traced here: 21.7 us
  Pallas kernels  21.1 us (96%)
  local copies, waits for them, and re-layouts  0.61 us (3%)
    pallas_call x1, Pallas kernels, body(): pl.pallas_call(functools.partial(kernel, feat, sub, chunk), out_shape=plt...  21.1 us
    unnamed x1, local copies, waits for them, and re-layouts  0.61 us

profile of v3, /device:TPU:0, one launch (start us, length us, event | category | flops | bytes accessed | tf_op | source)
XLA Modules:
  0.0 21.7 jit_solution(15625076827751107745)
XLA Ops:
  0.0 21.1 %shard_map.136 = bf16[4,2048]{1,0:T(4,128)(2,1)S(1)} custom-call(s32[4]{0:T(128)} %adapter_hbm.1, s32[4,4]{1,0:T(4,128)} %owner_hbm.1, s32[4]{0:T(128)} %length_hbm.1, bf16[16,2048]{1,0:T(8,128)(2,1)} %hidden_hbm.1, bf16[16,128]{1,0:T(8,128)(2,1)} %bitcast.1, f32[8,128]{1,0:T(8,128)} %constant.2.clone.freq_hbm, bf16[2048,1024]{1,0:T(8,128)(2,1)} %wq_hbm.1, ...), custom_call_target="tpu_custom_call" | custom-call | tf_op jit(solution)/shard_map/pallas_call | solution.py:518
  21.1 0.6 %copy.16 = bf16[4,2048]{1,0:T(4,128)(2,1)} copy(bf16[4,2048]{1,0:T(4,128)(2,1)S(1)} %shard_map.136) | data formatting | bytes 32768

commit v4 on v3

--- a/solution.py
+++ b/solution.py
@@ -229,10 +229,8 @@
     ld_wk.wait()
     ld_wv.wait()
     ld_down.wait()
-    ld_k = [
-        load(keys_hbm.at[s], keys.at[:, pl.ds(s * head, head)]) for s in range(slots)
-    ]
     ld_up = load(up_hbm, up)
+    ld_k = [load(keys_hbm.at[s], keys.at[s]) for s in range(slots)]
     part_k = jnp.dot(x, wk[...], preferred_element_type=f32)
     part_v = jnp.dot(x, wv[...], preferred_element_type=f32)
     lora = jnp.where(lora_mask, jnp.dot(x, down[...], preferred_element_type=f32), 0.0)
@@ -257,10 +255,7 @@
     for i in range(q_parts):
         ld_q[i].wait()
         if i == 0:
-            ld_v = [
-                load(values_hbm.at[s], values.at[:, pl.ds(s * head, head)])
-                for s in range(slots)
-            ]
+            ld_v = [load(values_hbm.at[s], values.at[s]) for s in range(slots)]
         if i == q_parts - 1:
             ld_o = [
                 load(
@@ -342,20 +337,22 @@
     draft = iota(shape, 1) - row_slot(shape) * DRAFT
     fresh = lax.dot_general(flat.astype(bf16), key_new, contract, preferred_element_type=f32)
     fresh = jnp.where((draft >= 0) & (draft <= (iota(shape, 0) & (DRAFT - 1))), fresh, -1e30)
-    shape = (slots * q_rows, chunk)
-    limit = jnp.full(shape, my_length[0], i32)
-    for k in range(1, slots):
-        limit = jnp.where(row_slot(shape) == k, my_length[k], limit)
-    top = fresh
+
+    def both(ref, c):
+        span = slice(c * chunk, (c + 1) * chunk)
+        return jnp.concatenate([ref[k, span, :] for k in range(slots)], axis=1)
+
+    tops = [fresh[k * q_rows : (k + 1) * q_rows] for k in range(slots)]
+    lane = iota((q_rows, chunk), 1)
     for c in range(chunks):
-        block = lax.dot_general(
-            queries, keys[c * chunk : (c + 1) * chunk, :], contract, preferred_element_type=f32
-        )
-        block = jnp.where(iota(shape, 1) + c * chunk < limit, block, -1e30)
-        scores[:, c * chunk : (c + 1) * chunk] = block
-        for i in range(chunk // LANES):
-            top = jnp.maximum(top, block[:, i * LANES : (i + 1) * LANES])
-    row_max = jnp.max(top, axis=1, keepdims=True)
+        block = lax.dot_general(queries, both(keys, c), contract, preferred_element_type=f32)
+        for k in range(slots):
+            part = block[k * q_rows : (k + 1) * q_rows]
+            part = jnp.where(lane < my_length[k] - c * chunk, part, -1e30)
+            scores[k * q_rows : (k + 1) * q_rows, c * chunk : (c + 1) * chunk] = part
+            for i in range(chunk // LANES):
+                tops[k] = jnp.maximum(tops[k], part[:, i * LANES : (i + 1) * LANES])
+    row_max = jnp.max(jnp.concatenate(tops, axis=0), axis=1, keepdims=True)
     weights = jnp.exp2((fresh - row_max) * factor)
     total = weights
     summed_new = jnp.dot(weights.astype(bf16), value_new, preferred_element_type=f32)
@@ -365,8 +362,7 @@
         for i in range(chunk // LANES):
             total = total + weights[:, i * LANES : (i + 1) * LANES]
         summed = summed + jnp.dot(
-            weights.astype(bf16), values[c * chunk : (c + 1) * chunk, :],
-            preferred_element_type=f32,
+            weights.astype(bf16), both(values, c), preferred_element_type=f32
         )
     denominator = jnp.sum(total, axis=1, keepdims=True)
     for s in range(slots):
@@ -472,7 +468,7 @@
     out_rows = tokens // sub
     q_parts = 2
     o_parts = 2
-    chunk = min(2048, context)
+    chunk = min(512, context)
     pieces = SUB16 // out_rows
     half = head // 2
     inv_freq = (rope_base ** (-(np.arange(half) * 2.0) / head)).astype(np.float32)
@@ -494,8 +490,8 @@
         V(adapter_down_weight.shape, bf16),
         V(adapter_up_weight.shape, bf16),
         V(output_weight.shape, bf16),
-        V((context, slots * head), bf16),
-        V((context, slots * head), bf16),
+        V(stored_keys.shape, bf16),
+        V(stored_values.shape, bf16),
         V((feat * rows, a_cols), f32),
         V((feat * rows, a_cols), f32),
         V((q_parts, feat * rows, query_cols // q_parts), f32),

time: 21.9 us -> 21.9 us (level)
  no operation moved by 1% of the time
where the time goes in v4:
time: 21.9 us; the launch traced here: 21.7 us
  Pallas kernels  21.1 us (96%)
  local copies, waits for them, and re-layouts  0.61 us (3%)
    pallas_call x1, Pallas kernels, body(): pl.pallas_call(functools.partial(kernel, feat, sub, chunk), out_shape=plt...  21.1 us
    unnamed x1, local copies, waits for them, and re-layouts  0.61 us

profile of v4, /device:TPU:0, one launch (start us, length us, event | category | flops | bytes accessed | tf_op | source)
XLA Modules:
  0.0 21.7 jit_solution(824359700704392120)
XLA Ops:
  0.0 21.1 %shard_map.136 = bf16[4,2048]{1,0:T(4,128)(2,1)S(1)} custom-call(s32[4]{0:T(128)} %adapter_hbm.1, s32[4,4]{1,0:T(4,128)} %owner_hbm.1, s32[4]{0:T(128)} %length_hbm.1, bf16[16,2048]{1,0:T(8,128)(2,1)} %hidden_hbm.1, bf16[16,128]{1,0:T(8,128)(2,1)} %bitcast.1, f32[8,128]{1,0:T(8,128)} %constant.2.clone.freq_hbm, bf16[2048,1024]{1,0:T(8,128)(2,1)} %wq_hbm.1, ...), custom_call_target="tpu_custom_call" | custom-call | tf_op jit(solution)/shard_map/pallas_call | solution.py:514
  21.1 0.6 %copy.16 = bf16[4,2048]{1,0:T(4,128)(2,1)} copy(bf16[4,2048]{1,0:T(4,128)(2,1)S(1)} %shard_map.136) | data formatting | bytes 32768

commit v5 on v4

--- a/solution.py
+++ b/solution.py
@@ -31,6 +31,7 @@
     feat,
     sub,
     chunk,
+    block_keys,
     adapter_hbm,
     owner_hbm,
     length_hbm,
@@ -251,7 +252,7 @@
                 {"feat": wrap(me + o, feat)},
             )
         )
-    ld_v = []
+    ld_v, own_q = [], []
     for i in range(q_parts):
         ld_q[i].wait()
         if i == 0:
@@ -264,16 +265,19 @@
                 )
                 for n in range(o_parts)
             ]
-        send_q[i] = jnp.dot(
-            x, wq[:, i * q_width : (i + 1) * q_width], preferred_element_type=f32
-        )
+        part = jnp.dot(x, wq[:, i * q_width : (i + 1) * q_width], preferred_element_type=f32)
+        own_q.append(part[0:rows])
         for o in range(1, feat):
-            block = pl.ds(o * rows, rows)
+            block = part[o * rows : (o + 1) * rows]
+            fold = q_width // halves
+            block = jnp.concatenate(
+                [block[:, h * fold : (h + 1) * fold] for h in range(halves)], axis=0
+            )
+            send_q[i, o] = block.astype(bf16)
             first.append(
                 send(
-                    send_q.at[i, block], recv_q.at[i, block],
-                    send_sem.at[1 + i, o], recv_sem.at[1 + i, o],
-                    {"feat": wrap(me + o, feat)},
+                    send_q.at[i, o], recv_q.at[i, o], send_sem.at[1 + i, o],
+                    recv_sem.at[1 + i, o], {"feat": wrap(me + o, feat)},
                 )
             )
     ld_up.wait()
@@ -305,9 +309,13 @@
     for copy in first[feat - 1 :]:
         copy.wait_recv()
     for i in range(q_parts):
-        total_q = send_q[i, 0:rows]
-        for o in range(1, feat):
-            total_q = total_q + recv_q[i, o * rows : (o + 1) * rows]
+        total_q = recv_q[i, 1].astype(f32)
+        for o in range(2, feat):
+            total_q = total_q + recv_q[i, o].astype(f32)
+        total_q = jnp.concatenate(
+            [total_q[h * rows : (h + 1) * rows] for h in range(halves)], axis=1
+        )
+        total_q = total_q + own_q[i]
         for g in range(q_width // head):
             whole_g = i * (q_width // head) + g
             part = total_q[:, g * head : (g + 1) * head]
@@ -322,7 +330,6 @@
     for copy in ld_k + ld_v:
         copy.wait()
     factor = head ** (-0.5) * LOG2E
-    chunks = context // chunk
     contract = (((1,), (1,)), ((), ()))
     queries = q_stage[...]
     flat = queries[:, 0:head]
@@ -342,28 +349,49 @@
         span = slice(c * chunk, (c + 1) * chunk)
         return jnp.concatenate([ref[k, span, :] for k in range(slots)], axis=1)
 
-    tops = [fresh[k * q_rows : (k + 1) * q_rows] for k in range(slots)]
     lane = iota((q_rows, chunk), 1)
-    for c in range(chunks):
-        block = lax.dot_general(queries, both(keys, c), contract, preferred_element_type=f32)
-        for k in range(slots):
-            part = block[k * q_rows : (k + 1) * q_rows]
-            part = jnp.where(lane < my_length[k] - c * chunk, part, -1e30)
-            scores[k * q_rows : (k + 1) * q_rows, c * chunk : (c + 1) * chunk] = part
+    per_block = block_keys // chunk
+    blocks = context // block_keys
+
+    def score_block(n):
+        tops = [jnp.full((q_rows, LANES), -1e30, f32) for k in range(slots)]
+        for c in range(n * per_block, (n + 1) * per_block):
+            block = lax.dot_general(queries, both(keys, c), contract, preferred_element_type=f32)
+            for k in range(slots):
+                part = block[k * q_rows : (k + 1) * q_rows]
+                part = jnp.where(lane < my_length[k] - c * chunk, part, -1e30)
+                scores[k * q_rows : (k + 1) * q_rows, c * chunk : (c + 1) * chunk] = part
+                for i in range(chunk // LANES):
+                    tops[k] = jnp.maximum(tops[k], part[:, i * LANES : (i + 1) * LANES])
+        return jnp.max(jnp.concatenate(tops, axis=0), axis=1, keepdims=True)
+
+    def weigh_block(n, block_max):
+        total, summed = None, None
+        for c in range(n * per_block, (n + 1) * per_block):
+            weights = jnp.exp2((scores[:, c * chunk : (c + 1) * chunk] - block_max) * factor)
             for i in range(chunk // LANES):
-                tops[k] = jnp.maximum(tops[k], part[:, i * LANES : (i + 1) * LANES])
-    row_max = jnp.max(jnp.concatenate(tops, axis=0), axis=1, keepdims=True)
+                part = weights[:, i * LANES : (i + 1) * LANES]
+                total = part if total is None else total + part
+            part = jnp.dot(weights.astype(bf16), both(values, c), preferred_element_type=f32)
+            summed = part if summed is None else summed + part
+        return total, summed
+
+    maxima, parts = [score_block(0)], []
+    for n in range(blocks):
+        if n + 1 < blocks:
+            maxima.append(score_block(n + 1))
+        parts.append(weigh_block(n, maxima[n]))
+    row_max = jnp.max(fresh, axis=1, keepdims=True)
+    for block_max in maxima:
+        row_max = jnp.maximum(row_max, block_max)
     weights = jnp.exp2((fresh - row_max) * factor)
     total = weights
     summed_new = jnp.dot(weights.astype(bf16), value_new, preferred_element_type=f32)
     summed = jnp.zeros((slots * q_rows, slots * head), f32)
-    for c in range(chunks):
-        weights = jnp.exp2((scores[:, c * chunk : (c + 1) * chunk] - row_max) * factor)
-        for i in range(chunk // LANES):
-            total = total + weights[:, i * LANES : (i + 1) * LANES]
-        summed = summed + jnp.dot(
-            weights.astype(bf16), both(values, c), preferred_element_type=f32
-        )
+    for n in range(blocks):
+        shrink = jnp.exp2((maxima[n] - row_max) * factor)
+        total = total + parts[n][0] * shrink
+        summed = summed + parts[n][1] * shrink
     denominator = jnp.sum(total, axis=1, keepdims=True)
     for s in range(slots):
         span = slice(s * q_rows, (s + 1) * q_rows)
@@ -469,6 +497,7 @@
     q_parts = 2
     o_parts = 2
     chunk = min(512, context)
+    block_keys = min(2048, context)
     pieces = SUB16 // out_rows
     half = head // 2
     inv_freq = (rope_base ** (-(np.arange(half) * 2.0) / head)).astype(np.float32)
@@ -494,8 +523,8 @@
         V(stored_values.shape, bf16),
         V((feat * rows, a_cols), f32),
         V((feat * rows, a_cols), f32),
-        V((q_parts, feat * rows, query_cols // q_parts), f32),
-        V((q_parts, feat * rows, query_cols // q_parts), f32),
+        V((q_parts, feat, SUB16, query_cols // q_parts * rows // SUB16), bf16),
+        V((q_parts, feat, SUB16, query_cols // q_parts * rows // SUB16), bf16),
         V((slots * query_cols // head * DRAFT, slots * head), f32),
         V((slots * query_cols // head * DRAFT, context), f32),
         V((SUB16, query_cols * rows // SUB16), f32),
@@ -512,7 +541,7 @@
         pltpu.SemaphoreType.DMA((o_parts, sub)),
     ]
     return pl.pallas_call(
-        functools.partial(kernel, feat, sub, chunk),
+        functools.partial(kernel, feat, sub, chunk, block_keys),
         out_shape=pltpu.VMEM((out_rows, out_cols), bf16),
         in_specs=[any_spec] * 14,
         out_specs=pl.BlockSpec(memory_space=pltpu.VMEM),

time: 21.9 us -> 20.7 us (0.945)
  Pallas kernels: 21.1 us -> 19.9 us
    pallas_call x1, Pallas kernels: 21.1 us -> 19.9 us  [body(): pl.pallas_call(functools.partial(kernel, feat, sub, chunk, block_keys), o...]
where the time goes in v5:
time: 20.7 us; the launch traced here: 20.5 us
  Pallas kernels  19.9 us (96%)
  local copies, waits for them, and re-layouts  0.61 us (3%)
    pallas_call x1, Pallas kernels, body(): pl.pallas_call(functools.partial(kernel, feat, sub, chunk, block_keys), o...  19.9 us
    unnamed x1, local copies, waits for them, and re-layouts  0.61 us

profile of v5, /device:TPU:0, one launch (start us, length us, event | category | flops | bytes accessed | tf_op | source)
XLA Modules:
  0.0 20.5 jit_solution(4101062853262441004)
XLA Ops:
  0.0 19.9 %shard_map.136 = bf16[4,2048]{1,0:T(4,128)(2,1)S(1)} custom-call(s32[4]{0:T(128)} %adapter_hbm.1, s32[4,4]{1,0:T(4,128)} %owner_hbm.1, s32[4]{0:T(128)} %length_hbm.1, bf16[16,2048]{1,0:T(8,128)(2,1)} %hidden_hbm.1, bf16[16,128]{1,0:T(8,128)(2,1)} %bitcast.1, f32[8,128]{1,0:T(8,128)} %constant.2.clone.freq_hbm, bf16[2048,1024]{1,0:T(8,128)(2,1)} %wq_hbm.1, ...), custom_call_target="tpu_custom_call" | custom-call | tf_op jit(solution)/shard_map/pallas_call | solution.py:543
  19.9 0.6 %copy.16 = bf16[4,2048]{1,0:T(4,128)(2,1)} copy(bf16[4,2048]{1,0:T(4,128)(2,1)S(1)} %shard_map.136) | data formatting | bytes 32768

commit v6 on v5

--- a/solution.py
+++ b/solution.py
@@ -197,7 +197,6 @@
     q_stage[...] = jnp.zeros_like(q_stage)
     ld_hidden.wait()
     ld_gain.wait()
-    ld_freq.wait()
     picked_hidden = jnp.dot(picks, hidden[...], preferred_element_type=f32)
     gains = gain[...].astype(f32)
     x = jnp.concatenate(
@@ -208,13 +207,6 @@
         axis=1,
     ).astype(bf16)
     squares = jnp.sum(picked_hidden * picked_hidden, axis=1, keepdims=True)
-
-    shape = (rows, head)
-    position = (slot_value(shape, my_length) + (iota(shape, 0) & (DRAFT - 1))).astype(f32)
-    angle = position * freq[...]
-    cosine = jnp.cos(angle)
-    sine = jnp.sin(angle)
-    sine = jnp.where(iota(shape, 1) < head // 2, -sine, sine)
 
     sends = []
 
@@ -280,6 +272,14 @@
                     recv_sem.at[1 + i, o], {"feat": wrap(me + o, feat)},
                 )
             )
+    ld_freq.wait()
+    shape = (rows, head)
+    position = (slot_value(shape, my_length) + (iota(shape, 0) & (DRAFT - 1))).astype(f32)
+    angle = position * freq[...]
+    cosine = jnp.cos(angle)
+    sine = jnp.sin(angle)
+    sine = jnp.where(iota(shape, 1) < head // 2, -sine, sine)
+
     ld_up.wait()
     for copy in first[: feat - 1]:
         copy.wait_recv()
@@ -327,7 +327,7 @@
                     s * DRAFT : (s + 1) * DRAFT
                 ]
 
-    for copy in ld_k + ld_v:
+    for copy in ld_k:
         copy.wait()
     factor = head ** (-0.5) * LOG2E
     contract = (((1,), (1,)), ((), ()))
@@ -380,6 +380,9 @@
     for n in range(blocks):
         if n + 1 < blocks:
             maxima.append(score_block(n + 1))
+        if n == 0:
+            for copy in ld_v:
+                copy.wait()
         parts.append(weigh_block(n, maxima[n]))
     row_max = jnp.max(fresh, axis=1, keepdims=True)
     for block_max in maxima:

time: 20.7 us -> 20.7 us (level)
  no operation moved by 1% of the time
where the time goes in v6:
time: 20.7 us; the launch traced here: 20.6 us
  Pallas kernels  20 us (97%)
  local copies, waits for them, and re-layouts  0.61 us (3%)
    pallas_call x1, Pallas kernels, body(): pl.pallas_call(functools.partial(kernel, feat, sub, chunk, block_keys), o...  20 us
    unnamed x1, local copies, waits for them, and re-layouts  0.61 us

profile of v6, /device:TPU:0, one launch (start us, length us, event | category | flops | bytes accessed | tf_op | source)
XLA Modules:
  0.0 20.6 jit_solution(5549310208913769274)
XLA Ops:
  0.0 20.0 %shard_map.136 = bf16[4,2048]{1,0:T(4,128)(2,1)S(1)} custom-call(s32[4]{0:T(128)} %adapter_hbm.1, s32[4,4]{1,0:T(4,128)} %owner_hbm.1, s32[4]{0:T(128)} %length_hbm.1, bf16[16,2048]{1,0:T(8,128)(2,1)} %hidden_hbm.1, bf16[16,128]{1,0:T(8,128)(2,1)} %bitcast.1, f32[8,128]{1,0:T(8,128)} %constant.2.clone.freq_hbm, bf16[2048,1024]{1,0:T(8,128)(2,1)} %wq_hbm.1, ...), custom_call_target="tpu_custom_call" | custom-call | tf_op jit(solution)/shard_map/pallas_call | solution.py:546
  20.0 0.6 %copy.16 = bf16[4,2048]{1,0:T(4,128)(2,1)} copy(bf16[4,2048]{1,0:T(4,128)(2,1)S(1)} %shard_map.136) | data formatting | bytes 32768

commit v7 on v5

--- a/solution.py
+++ b/solution.py
@@ -495,7 +495,7 @@
     out_cols = output_weight.shape[1]
     out_rows = tokens // sub
     q_parts = 2
-    o_parts = 2
+    o_parts = 1
     chunk = min(512, context)
     block_keys = min(2048, context)
     pieces = SUB16 // out_rows

time: 20.7 us -> 20.6 us (level)
  no operation moved by 1% of the time
where the time goes in v7:
time: 20.6 us; the launch traced here: 20.4 us
  Pallas kernels  19.8 us (96%)
  local copies, waits for them, and re-layouts  0.61 us (3%)
    pallas_call x1, Pallas kernels, body(): pl.pallas_call(functools.partial(kernel, feat, sub, chunk, block_keys), o...  19.8 us
    unnamed x1, local copies, waits for them, and re-layouts  0.61 us

profile of v7, /device:TPU:0, one launch (start us, length us, event | category | flops | bytes accessed | tf_op | source)
XLA Modules:
  0.0 20.4 jit_solution(1912537464469562668)
XLA Ops:
  0.0 19.8 %shard_map.136 = bf16[4,2048]{1,0:T(4,128)(2,1)S(1)} custom-call(s32[4]{0:T(128)} %adapter_hbm.1, s32[4,4]{1,0:T(4,128)} %owner_hbm.1, s32[4]{0:T(128)} %length_hbm.1, bf16[16,2048]{1,0:T(8,128)(2,1)} %hidden_hbm.1, bf16[16,128]{1,0:T(8,128)(2,1)} %bitcast.1, f32[8,128]{1,0:T(8,128)} %constant.2.clone.freq_hbm, bf16[2048,1024]{1,0:T(8,128)(2,1)} %wq_hbm.1, ...), custom_call_target="tpu_custom_call" | custom-call | tf_op jit(solution)/shard_map/pallas_call | solution.py:543
  19.8 0.6 %copy.16 = bf16[4,2048]{1,0:T(4,128)(2,1)} copy(bf16[4,2048]{1,0:T(4,128)(2,1)S(1)} %shard_map.136) | data formatting | bytes 32768
